TPU v7x, 32 devices: a whole 2x2x4 slice. The times are simulated.
32 devices in a mesh: groups: 2 (over y), tile: 4 (over z), segment: 2 (over core), mp: 2 (over x).
Axes of the slice: x: 2, y: 2, z: 4, core: 2. Of those that a mesh axis runs over, the one named last changes fastest.
Arguments:
- spectra: bfloat16 [2, 64, 48, 224], P(None, ('groups', 'tile')), parts along dimension 1, may hold values from -6 to 6
- valid: int32 [2, 64], P(None, 'groups'), parts along dimension 1, may hold values from 1 to 48, as said below
- project: bfloat16 [224, 16], replicated, may hold values from -0.375 to 0.375
- enc_in: bfloat16 [768, 3072], P(None, 'mp'), may hold values from -0.21875 to 0.21875
- enc_out: bfloat16 [3072, 768], P('mp'), may hold values from -0.109375 to 0.109375
- tok_embed: bfloat16 [48, 2048], replicated, may hold values from -0.875 to 0.875
- band_embed: bfloat16 [16, 2048], P('tile'), may hold values from -3 to 3
- dec_in: bfloat16 [2048, 8192], P('tile', 'mp'), may hold values from -0.125 to 0.125
- dec_out: bfloat16 [8192, 2048], P('mp', 'tile'), may hold values from -0.0625 to 0.0625
- head: bfloat16 [2048, 672], P('tile', 'mp'), may hold values from -0.125 to 0.125
Outputs:
- grad_project: float32 [448, 16], P(('groups', 'tile', 'segment')), parts along dimension 0
- grad_enc_in: float32 [1536, 3072], P(('groups', 'tile', 'segment'), 'mp'), parts along dimension 0
- grad_enc_out: float32 [6144, 768], P(('groups', 'mp'), ('tile', 'segment')), parts along dimension 0
There are 2 independent parts, one for each index of `groups`. A program takes and returns all parts, laid end to end along the dimension named above; an argument that names none is the same for every part. Nothing has to cross between parts.
Inputs may be any that keep to these rules, and one draw needn't show every extreme that they name: Pixels of patch n in micro-batch m with index below valid[m, n] count in the loss.
All inputs are finite; a program needn't handle non-finite values.
Results may differ from a plain program's by a relative error of at most 0.018.
Values may be sent and summed in bfloat16 or wider, within the bound.
A program may use at most 128 MiB of HBM per device.

v0:
```python
import jax
import jax.numpy as jnp
from jax import lax
from jax.sharding import PartitionSpec as P

BF = jnp.bfloat16
F32 = jnp.float32


def inv_rms(values):
    return lax.rsqrt(jnp.mean(values * values, axis=-1, keepdims=True) + 1e-05)


def rms_back(values, gradient):
    scaling = inv_rms(values)
    normed = values * scaling
    return scaling * (gradient - normed * jnp.mean(gradient * normed, axis=-1, keepdims=True))


def gelu(v):
    return 0.5 * v * (1 + jnp.tanh(0.7978845608028654 * (v + 0.044715 * v * v * v)))


def gelu_and_slope(v):
    square = v * v
    t = jnp.tanh(0.7978845608028654 * v * (1 + 0.044715 * square))
    half = 0.5 * (1 + t)
    slope = half + 0.5 * v * (1 - t * t) * 0.7978845608028654 * (1 + 3 * 0.044715 * square)
    return (v * half, slope)


def dot(a, b):
    return jnp.dot(a, b, preferred_element_type=F32)


def dot_t(a, b):
    return lax.dot_general(a, b, (((1,), (1,)), ((), ())), preferred_element_type=F32)


def t_dot(a, b):
    return lax.dot_general(a, b, (((0,), (0,)), ((), ())), preferred_element_type=F32)


def body(spectra, valid, project, enc_in, enc_out, tok_embed, band_embed, dec_in, dec_out, head):
    tile, seg, mp = (lax.axis_index(a) for a in ("tile", "segment", "mp"))
    T, S, M = (lax.axis_size(a) for a in ("tile", "segment", "mp"))
    batches, per_tile, pixels, bands = spectra.shape
    codes = project.shape[1]
    width = bands // codes
    local = batches * per_tile
    share = local // (S * M)
    rows = T * local
    student = codes * pixels
    dim = tok_embed.shape[1]
    dt = dec_in.shape[0]
    hid = dec_in.shape[1] // S
    once = jnp.logical_and(seg == 0, mp == 0).astype(F32)
    patches = spectra.reshape(local, pixels, bands)
    flat = patches.reshape(local * pixels, bands)
    feat_local = (
        dot(flat, project)
        .astype(BF)
        .reshape(local, pixels, codes)
        .transpose(0, 2, 1)
        .reshape(local, student)
    )
    feats = lax.all_gather(feat_local, "tile")
    feats = feats.reshape(T, S, M, share, student).transpose(1, 2, 0, 3, 4).reshape(rows, student)
    band_all = lax.all_gather(band_embed, "tile", tiled=True)
    head_full = lax.all_gather(head, "mp", axis=1, tiled=True)
    embed = jnp.concatenate([tok_embed, band_all], axis=0)
    embed_z = lax.dynamic_slice_in_dim(embed, tile * dt, dt, 1)
    d_in = lax.dynamic_slice_in_dim(dec_in, seg * hid, hid, 1)
    d_out = lax.dynamic_slice_in_dim(dec_out, seg * hid, hid, 0)
    folded = lax.psum(dot(embed_z, d_in).astype(BF), "tile")
    fold_tok, fold_band = (folded[:pixels], folded[pixels:])
    feats32 = feats.astype(F32)
    normed = (feats32 * inv_rms(feats32)).astype(BF)
    pre_act, pre_slope = gelu_and_slope(dot(normed, enc_in))
    act_out = pre_act.astype(BF)
    summed = lax.psum(dot(act_out, enc_out).astype(BF), "mp").astype(F32)
    encoded = (feats32 + summed).astype(BF)
    tokens = rows * codes
    tok = encoded.reshape(tokens, pixels)
    embedded = (
        (dot(tok, tok_embed).reshape(rows, codes, dim) + band_all.astype(F32))
        .reshape(tokens, dim)
        .astype(BF)
    )
    scaling = inv_rms(embedded.astype(F32))
    hid_pre = scaling * (
        dot(tok, fold_tok).reshape(rows, codes, hid) + fold_band.astype(F32)
    ).reshape(tokens, hid)
    hid_act, hid_slope = gelu_and_slope(hid_pre)
    embedded_z = lax.dynamic_slice_in_dim(embedded, tile * dt, dt, 1)
    decoded = (once * embedded_z.astype(F32) + dot(hid_act.astype(BF), d_out)).astype(BF)
    partial = dot(decoded, head_full).astype(BF)
    own = lax.psum_scatter(
        partial.reshape(S * M, T, share * codes, -1), ("segment", "mp"), scatter_dimension=0
    )
    own = lax.psum_scatter(own, "tile", scatter_dimension=0).astype(F32)
    quarter = (seg * M + mp) * share
    own_patches = lax.dynamic_slice_in_dim(patches, quarter, share, 0)
    target = (
        own_patches.reshape(share, pixels, codes, width)
        .transpose(0, 2, 1, 3)
        .reshape(share * codes, -1)
    )
    total_valid = jnp.sum(valid.astype(F32))
    loss_scale = 2.0 * batches * valid.shape[1] / total_valid
    own_valid = lax.dynamic_slice_in_dim(valid, tile * per_tile, per_tile, 1).reshape(local)
    own_valid = lax.dynamic_slice_in_dim(own_valid, quarter, share, 0)
    column = jnp.arange(pixels * width, dtype=jnp.int32) // width
    mask = (column[None, :] < jnp.repeat(own_valid, codes)[:, None]).astype(F32)
    grad_own = (loss_scale * mask * (own - target.astype(F32))).astype(BF)
    grad_rebuilt = lax.all_gather(lax.all_gather(grad_own, "tile"), ("segment", "mp")).reshape(
        tokens, -1
    )
    grad_decoded = dot_t(grad_rebuilt, head_full).astype(BF)
    grad_hid = hid_slope * dot_t(grad_decoded, d_out)
    tok_z = lax.dynamic_slice_in_dim(tok_embed, tile * dt, dt, 1)
    unit_tok = dot_t((embedded.astype(F32) * scaling).astype(BF), tok_embed)
    along = jnp.sum(grad_hid * hid_pre, axis=1, keepdims=True) / dim
    grad_tok = scaling * (dot_t(grad_hid.astype(BF), fold_tok) - unit_tok * along)
    grad_tok = grad_tok + once * dot_t(grad_decoded, tok_z)
    grad_encoded = lax.psum(grad_tok.reshape(rows, student).astype(BF), ("tile", "segment", "mp"))
    grad_act = (pre_slope * dot_t(grad_encoded, enc_out)).astype(BF)
    columns = student // (T * S)
    start = (tile * S + seg) * columns
    grad_out = t_dot(act_out, lax.dynamic_slice_in_dim(grad_encoded, start, columns, 1))
    grad_in = t_dot(lax.dynamic_slice_in_dim(normed, start, columns, 1), grad_act)
    grad_normed = lax.psum(dot_t(grad_act, enc_in).astype(BF), "mp").astype(F32)
    own_rows = lambda a: lax.dynamic_slice_in_dim(
        a.reshape(S * M, T, share, student), tile, 1, 1
    ).reshape(local, student)
    grad_feat = (
        own_rows(grad_encoded).astype(F32) + rms_back(feat_local.astype(F32), own_rows(grad_normed))
    ).astype(BF)
    grad_codes = grad_feat.reshape(local, codes, pixels).transpose(0, 2, 1).reshape(-1, codes)
    grad_proj = jnp.sum(lax.all_gather(t_dot(flat, grad_codes), "tile"), axis=0)
    proj_rows = bands // (T * S)
    grad_proj = lax.dynamic_slice_in_dim(grad_proj, (tile * S + seg) * proj_rows, proj_rows, 0)
    return (grad_proj, grad_in, grad_out)


def solution(mesh):
    placed = (
        P(None, ("groups", "tile"), None, None),
        P(None, "groups"),
        P(),
        P(None, "mp"),
        P("mp", None),
        P(),
        P("tile", None),
        P("tile", "mp"),
        P("mp", "tile"),
        P("tile", "mp"),
    )
    return jax.shard_map(
        body,
        mesh=mesh,
        in_specs=placed,
        out_specs=(
            P(("groups", "tile", "segment"), None),
            P(("groups", "tile", "segment"), "mp"),
            P(("groups", "mp"), ("tile", "segment")),
        ),
        check_vma=False,
    )
```

profile of v0, /device:TPU:0, one launch (start us, length us, event | category | flops | bytes accessed | tf_op | source)
XLA Modules:
  0.0 350.5 jit_solution(10092934858017082224)
XLA Ops:
  7.2 1.4 convolution_convert_fusion.5
  8.6 0.2 reshape.254
  8.8 0.7 fusion.49
  9.4 0.1 all_gather_reshape.3
  9.6 15.0 %all_gather.25 = bf16[4,16,768]{2,1,0:T(8,128)(2,1)S(1)} all-gather(bf16[1,16,768]{2,1,0:T(8,128)(2,1)S(1)} %all_gather_reshape.3), channel_id=1, replica_groups=mesh['groups'=2,'tile'=4,'segment'=2,'mp'=2] {'tile'}, dimensions={0}, use_global_device_ids=true | all-gather | bytes 122880 | tf_op jit(solution)/shard_map/all_gather | solution.py:67
  24.7 0.1 multiply_reduce_fusion.2
  25.0 0.1 rsqrt.35
  25.1 0.1 multiply_convert_fusion.7
  25.2 2.2 fusion.50
  27.4 0.7 copy-done.3
  28.2 1.2 convolution_convert_fusion.4
  29.5 13.3 %all-gather.2 = bf16[4,4,2048]{2,1,0:T(4,128)(2,1)S(1)} all-gather(bf16[1,4,2048]{2,1,0:T(4,128)(2,1)S(1)} %bitcast.88), channel_id=1, replica_groups=mesh['groups'=2,'tile'=4,'segment'=2,'mp'=2] {'tile'}, dimensions={0}, use_global_device_ids=true | all-gather | bytes 81920 | tf_op jit(solution)/shard_map/all_gather | solution.py:69
  42.8 2.8 convolution_convert_fusion
  45.7 0.7 convert_element_type.165
  46.4 8.4 %all_gather.27 = bf16[512,672]{0,1:T(8,128)(2,1)S(1)} all-gather(bf16[512,336]{0,1:T(8,128)(2,1)} %param.19), channel_id=1, replica_groups=mesh['groups'=2,'tile'=4,'segment'=2,'mp'=2] {'mp'}, dimensions={1}, use_global_device_ids=true | all-gather | bytes 1032192 | tf_op jit(solution)/shard_map/all_gather | solution.py:70
  54.7 1.0 add_convert_fusion.2
  55.8 0.3 dot_general.61
  56.1 4.2 %multiply_reduce_fusion.1 = (f32[64,16]{1,0:T(8,128)S(1)}, bf16[64,16,2048]{2,1,0:T(8,128)(2,1)}) fusion(f32[16,2048]{1,0:T(8,128)} %convert_element_type.165, bf16[64,16,48]{2,1,0:T(8,128)(2,1)S(1)} %dot_general.61, bf16[48,2048]{1,0:T(8,128)(2,1)} %param.15), kind=kOutput, calls=%fused_computation.7 | convolution fusion | flops 211811328 | bytes 4624384 | tf_op jit(solution)/shard_map/dot_general | solution.py:33
  60.4 29.6 %all-reduce.7.cloned.1.call-done = bf16[64,2048]{1,0:T(8,128)(2,1)} async-done(((bf16[64,2048]{1,0:T(8,128)(2,1)}), bf16[64,2048]{1,0:T(8,128)(2,1)}) %all-reduce.7.cloned.1.call-update) | async-done | bytes 262160 | tf_op jit(solution)/shard_map/psum | solution.py:75
  90.0 0.8 slice_convert_fusion
  90.8 2.2 convolution_add_fusion
  93.0 5.3 %multiply_convert_fusion.1 = bf16[1024,2048]{1,0:T(8,128)(2,1)} fusion(f32[64,16,2048]{2,1,0:T(8,128)S(1)} %convolution_add_fusion, f32[1024]{0:T(1024)S(1)} %rsqrt.37), kind=kLoop, calls=%fused_computation.3 | loop fusion | flops 20971520 | bytes 12587008 | tf_op jit(solution)/shard_map/convert_element_type | solution.py:96
  98.3 7.2 %convolution_convert_fusion.1 = bf16[1024,672]{0,1:T(8,128)(2,1)} fusion(bf16[512,672]{0,1:T(8,128)(2,1)S(1)} %all_gather.27, bf16[1024,2048]{1,0:T(8,128)(2,1)} %multiply_convert_fusion.1, bf16[4096,512]{1,0:T(8,128)(2,1)} %param.18, s32[]{:T(128)S(6)} %select_n.37, bf16[1024,2048]{1,0:T(8,128)(2,1)} %bitcast.90, s32[]{:T(128)S(6)} %select_n.36, ...), kind=kOutput, calls=%fused_computation.22 | convolution fusion | flops 2854912000 | bytes 9404428 | tf_op jit(solution)/shard_map/dot_general | solution.py:33
  105.5 2.6 copy.40
  108.2 28.0 %reduce-scatter.3.cloned.1.call-done = bf16[1,4,64,672]{3,2,1,0:T(8,128)(2,1)} async-done(((bf16[4,4,64,672]{3,2,1,0:T(8,128)(2,1)}), bf16[1,4,64,672]{3,2,1,0:T(8,128)(2,1)}) %reduce-scatter.3.cloned.1.call-update) | async-done | bytes 344080 | tf_op jit(solution)/shard_map/reduce_scatter | solution.py:98
  136.6 0.1 lt.54
  136.7 0.2 copy.49
  136.9 1.8 copy.42
  138.7 1.9 reshape.268
  140.7 0.6 convert_reduce_fusion
  142.0 17.0 %reduce-scatter.5.cloned.1.call-done = bf16[1,64,672]{2,1,0:T(8,128)(2,1)} async-done(((bf16[4,64,672]{2,1,0:T(8,128)(2,1)}), bf16[1,64,672]{2,1,0:T(8,128)(2,1)}) %reduce-scatter.5.cloned.1.call-update) | async-done | bytes 86032 | tf_op jit(solution)/shard_map/reduce_scatter | solution.py:101
  159.0 1.0 multiply_convert_fusion.6
  160.0 15.8 %all_gather.28 = bf16[4,64,672]{2,1,0:T(8,128)(2,1)} all-gather(bf16[1,64,672]{2,1,0:T(8,128)(2,1)S(1)} %multiply_convert_fusion.6), channel_id=1, replica_groups=mesh['groups'=2,'tile'=4,'segment'=2,'mp'=2] {'tile'}, dimensions={0}, use_global_device_ids=true | all-gather | bytes 430080 | tf_op jit(solution)/shard_map/all_gather | solution.py:116
  175.8 0.2 all-reduce.9.cloned.1.call-start
  176.0 0.2 multiply_reduce_fusion.3
  176.2 17.2 %all-gather.6.cloned.1.call-done = bf16[16,64,672]{2,1,0:T(8,128)(2,1)} async-done(((bf16[4,64,672]{2,1,0:T(8,128)(2,1)}), bf16[16,64,672]{2,1,0:T(8,128)(2,1)}) %all-gather.6.cloned.1.call-update) | async-done | bytes 1376272 | tf_op jit(solution)/shard_map/all_gather | solution.py:116
  193.4 2.7 convolution_convert_fusion.2
  196.1 0.2 copy-done.12
  196.3 9.2 %multiply_reduce_fusion = (f32[1024]{0:T(1024)S(1)}, bf16[1024,2048]{1,0:T(8,128)(2,1)S(1)}) fusion(f32[64,16,2048]{2,1,0:T(8,128)} %copy-done.1, f32[1024]{0:T(1024)S(1)} %rsqrt.37, bf16[1024,512]{1,0:T(8,128)(2,1)S(1)} %convolution_convert_fusion.2, bf16[4096,512]{1,0:T(8,128)(2,1)S(1)} %copy-done.12, s32[]{:T(128)S(6)} %select_n.37), kind=kOutput, calls=%fused_computation.1 | convolution fusion | flops 2191522816 | bytes 15736836 | tf_op jit(solution)/shard_map/dot_general | solution.py:37
  205.5 0.4 convolution_multiply_fusion.1
  206.0 1.5 fusion.20
  207.5 2.0 fusion.21
  209.5 1.1 copy.43
  210.6 0.9 convert_element_type.188
  211.6 1.0 reshape.270
  212.7 86.1 %all-reduce.9.cloned.1.call-done = bf16[64,768]{1,0:T(8,128)(2,1)} async-done(((bf16[64,768]{1,0:T(8,128)(2,1)}), bf16[64,768]{1,0:T(8,128)(2,1)}) %all-reduce.9.cloned.1.call-update) | async-done | bytes 98320 | tf_op jit(solution)/shard_map/psum | solution.py:126
  298.8 1.7 fusion.4
  300.5 3.1 convolution_convert_fusion.3
  303.7 1.9 fusion.36
  305.6 0.9 reshape.261
  306.5 0.7 copy.45
  307.2 1.9 fusion.34
  309.1 0.9 reshape.260
  310.1 0.1 reshape.269
  310.2 17.2 %all-reduce.11.cloned.1.call-done = bf16[4,4,4,768]{3,2,0,1:T(4,128)(2,1)} async-done(((bf16[4,4,4,768]{3,2,0,1:T(4,128)(2,1)}), bf16[4,4,4,768]{3,2,0,1:T(4,128)(2,1)}) %all-reduce.11.cloned.1.call-update) | async-done | bytes 98320 | tf_op jit(solution)/shard_map/psum | solution.py:132
  327.4 0.9 multiply_reduce_fusion.4
  328.3 0.1 div.44
  328.4 0.7 dynamic-slice_convert_fusion.1
  329.1 0.1 reshape.263
  329.2 0.1 fusion.30
  329.4 0.1 reshape.264
  329.5 0.1 convolution_bitcast_fusion
  329.7 13.3 %all-gather.3 = f32[4,224,16]{1,2,0:T(8,128)S(1)} all-gather(f32[1,224,16]{1,2,0:T(8,128)S(1)} %convolution_bitcast_fusion), channel_id=3, replica_groups=mesh['groups'=2,'tile'=4,'segment'=2,'mp'=2] {'tile'}, dimensions={0}, use_global_device_ids=true | all-gather | bytes 71680 | tf_op jit(solution)/shard_map/all_gather | solution.py:140
  342.9 0.7 constant_dynamic-slice_fusion
  (62 shorter events, 1.3 us)
Async XLA Ops:
  7.2 21.0 %copy-start = (bf16[1536,768]{1,0:T(8,128)(2,1)S(1)}, bf16[1536,768]{1,0:T(8,128)(2,1)}, u32[]{:S(2)}) copy-start(bf16[1536,768]{1,0:T(8,128)(2,1)} %param.14) | copy-start | bytes 7077892
  7.2 22.3 %copy-start.10 = (bf16[4,2048]{1,0:T(4,128)(2,1)S(1)}, bf16[4,2048]{1,0:T(4,128)(2,1)}, u32[]{:S(2)}) copy-start(bf16[4,2048]{1,0:T(4,128)(2,1)} %param.16) | copy-start | bytes 49156
  7.2 47.6 %all-reduce.5.cloned.1.call-start = ((), (), s32[]{:S(2)}) async-start(), calls=%async_computation.2 | async-start | bytes 196608 | tf_op jit(solution)/shard_map/psum | solution.py:81
  7.2 35.6 %copy-start.8 = (bf16[48,2048]{1,0:T(8,128)(2,1)S(1)}, bf16[48,2048]{1,0:T(8,128)(2,1)}, u32[]{:S(2)}) copy-start(bf16[48,2048]{1,0:T(8,128)(2,1)} %param.15) | copy-start | bytes 589828
  25.2 4.3 %copy-start.7 = (bf16[64,768]{1,0:T(8,128)(2,1)}, bf16[64,768]{1,0:T(8,128)(2,1)S(1)}, u32[]{:S(2)}) copy-start(bf16[64,768]{1,0:T(8,128)(2,1)S(1)} %multiply_convert_fusion.7) | copy-start | bytes 294916
  27.4 0.8 copy-start.3
  29.4 60.6 %all-reduce.7.cloned.1.call-start = ((), (), s32[]{:S(2)}) async-start(), calls=%async_computation.3 | async-start | bytes 524288 | tf_op jit(solution)/shard_map/psum | solution.py:75
  45.6 90.6 %reduce-scatter.3.cloned.1.call-start = ((), (), s32[]{:S(2)}) async-start(), calls=%async_computation.4 | async-start | bytes 1966080 | tf_op jit(solution)/shard_map/reduce_scatter | solution.py:98
  54.7 43.5 %copy-start.6 = (bf16[512,672]{0,1:T(8,128)(2,1)}, bf16[512,672]{0,1:T(8,128)(2,1)S(1)}, u32[]{:S(2)}) copy-start(bf16[512,672]{0,1:T(8,128)(2,1)S(1)} %all_gather.27) | copy-start | bytes 2064388
  93.0 5.3 %copy-start.1 = (f32[64,16,2048]{2,1,0:T(8,128)}, f32[64,16,2048]{2,1,0:T(8,128)S(1)}, u32[]{:S(2)}) copy-start(f32[64,16,2048]{2,1,0:T(8,128)S(1)} %convolution_add_fusion) | copy-start | bytes 25165828
  105.5 30.8 %copy-start.11 = (s32[2,32]{1,0:T(2,128)S(1)}, s32[2,32]{1,0:T(2,128)}, u32[]{:S(2)}) copy-start(s32[2,32]{1,0:T(2,128)} %param.11) | copy-start | bytes 772
  105.5 31.2 %copy-start.2 = (bf16[2,8,48,224]{3,2,1,0:T(8,128)(2,1)S(1)}, bf16[2,8,48,224]{3,2,1,0:T(8,128)(2,1)}, u32[]{:S(2)}) copy-start(bf16[2,8,48,224]{3,2,1,0:T(8,128)(2,1)} %param.10) | copy-start | bytes 1032196
  108.1 50.8 %reduce-scatter.5.cloned.1.call-start = ((), (), s32[]{:S(2)}) async-start(), calls=%async_computation.5 | async-start | bytes 491520 | tf_op jit(solution)/shard_map/reduce_scatter | solution.py:101
  136.2 57.2 %all-gather.6.cloned.1.call-start = ((), (), s32[]{:S(2)}) async-start(), calls=%async_computation.8 | async-start | bytes 1966080 | tf_op jit(solution)/shard_map/all_gather | solution.py:116
  175.8 123.0 %all-reduce.9.cloned.1.call-start = ((), (), s32[]{:S(2)}) async-start(), calls=%async_computation.6 | async-start | bytes 196608 | tf_op jit(solution)/shard_map/psum | solution.py:126
  193.4 2.9 copy-start.12
  196.3 9.2 %copy-start.9 = (bf16[48,2048]{1,0:T(8,128)(2,1)S(1)}, bf16[48,2048]{1,0:T(8,128)(2,1)}, u32[]{:S(2)}) copy-start(bf16[48,2048]{1,0:T(8,128)(2,1)} %param.15) | copy-start | bytes 589828
  196.3 9.7 %copy-start.13 = (bf16[64,16,2048]{2,1,0:T(8,128)(2,1)S(1)}, bf16[64,16,2048]{2,1,0:T(8,128)(2,1)}, u32[]{:S(2)}) copy-start(bf16[64,16,2048]{2,1,0:T(8,128)(2,1)} %get-tuple-element.6) | copy-start | bytes 12582916
  206.0 1.5 copy-start.5
  207.5 91.4 %copy-start.4 = (f32[64,1536]{1,0:T(8,128)S(1)}, f32[64,1536]{1,0:T(8,128)}, u32[]{:S(2)}) copy-start(f32[64,1536]{1,0:T(8,128)} %copy-done.3) | copy-start | bytes 1179652
  211.5 115.9 %all-reduce.11.cloned.1.call-start = ((), (), s32[]{:S(2)}) async-start(), calls=%async_computation.7 | async-start | bytes 196608 | tf_op jit(solution)/shard_map/psum | solution.py:132
Sparse Core Ops, SparseCore 0:
  29.5 22.1 all-reduce.4
  54.6 35.3 all-reduce.6
  108.3 27.9 reduce-scatter.2
  138.3 20.5 reduce-scatter.4
  175.9 17.4 all-gather.5
  211.6 87.1 all-reduce.8
  307.3 20.0 all-reduce.10
where the time goes:
time: 351 us; the launch traced here: 350 us
  waiting for transfers between devices  195 us (56%)
  blocking collectives  65.8 us (19%)
  matrix products  45.8 us (13%)
  local copies, waits for them, and re-layouts  15.7 us (4%)
  between operations  15.2 us (4%)
  other arithmetic  12.3 us (4%)
    psum x1, waiting for transfers between devices, body(): lax.psum(grad_tok.reshape(rows, student).astype(BF), ('tile', 'segment',...  86.1 us
    psum x1, waiting for transfers between devices, body(): folded = lax.psum(dot(embed_z, d_in).astype(BF), 'tile')  29.6 us
    reduce_scatter x1, waiting for transfers between devices, body(): lax.psum_scatter(partial.reshape(S * M, T, share * codes, -1), ('segment'...  28 us
    dot_general x7, matrix products, dot(): return jnp.dot(a, b, preferred_element_type=F32)  21.1 us
    dot_general x7, matrix products, dot_t(): lax.dot_general(a, b, (((1,), (1,)), ((), ())), preferred_element_type=F32)  20.7 us
    all_gather x1, waiting for transfers between devices, body(): lax.all_gather(lax.all_gather(grad_own, 'tile'), ('segment', 'mp'))  17.2 us
    psum x1, waiting for transfers between devices, body(): grad_normed = lax.psum(dot_t(grad_act, enc_in).astype(BF), 'mp').astype(F32)  17.2 us
    reduce_scatter x1, waiting for transfers between devices, body(): own = lax.psum_scatter(own, 'tile', scatter_dimension=0).astype(F32)  17 us
  transfers between devices with their start and end apart: 7, of which 6 were waited for; matrix products, arithmetic and copies ran while one was open for 5% of the time, Pallas kernels for 0%

commit v1 on v0

--- a/solution.py
+++ b/solution.py
@@ -123,7 +123,8 @@
     along = jnp.sum(grad_hid * hid_pre, axis=1, keepdims=True) / dim
     grad_tok = scaling * (dot_t(grad_hid.astype(BF), fold_tok) - unit_tok * along)
     grad_tok = grad_tok + once * dot_t(grad_decoded, tok_z)
-    grad_encoded = lax.psum(grad_tok.reshape(rows, student).astype(BF), ("tile", "segment", "mp"))
+    inner = lax.psum(grad_tok.reshape(rows, student).astype(BF), ("segment", "mp"))
+    grad_encoded = lax.psum(inner, "tile")
     grad_act = (pre_slope * dot_t(grad_encoded, enc_out)).astype(BF)
     columns = student // (T * S)
     start = (tile * S + seg) * columns

time: 351 us -> 333 us (0.949)
  waiting for transfers between devices: 195 us -> 177 us
    psum x1 -> x2, waiting for transfers between devices: 86.1 us -> 66.5 us  [the longest x1 35.4 us: body(): grad_encoded = lax.psum(inner, 'tile')]
  transfers between devices with their start and end apart: 7 -> 8, of which waited for: 6 -> 7; matrix products, arithmetic and copies ran while one was open for 5% -> 6% of each run, Pallas kernels for 0% -> 0%
where the time goes in v1:
time: 333 us; the launch traced here: 332 us
  waiting for transfers between devices  177 us (53%)
  blocking collectives  65.8 us (20%)
  matrix products  45.8 us (14%)
  local copies, waits for them, and re-layouts  15.7 us (5%)
  between operations  15.2 us (5%)
  other arithmetic  12.3 us (4%)
    psum x1, waiting for transfers between devices, body(): grad_encoded = lax.psum(inner, 'tile')  35.4 us
    psum x1, waiting for transfers between devices, body(): lax.psum(grad_tok.reshape(rows, student).astype(BF), ('segment', 'mp'))  31.1 us
    psum x1, waiting for transfers between devices, body(): folded = lax.psum(dot(embed_z, d_in).astype(BF), 'tile')  29.6 us
    reduce_scatter x1, waiting for transfers between devices, body(): lax.psum_scatter(partial.reshape(S * M, T, share * codes, -1), ('segment'...  28 us
    dot_general x7, matrix products, dot(): return jnp.dot(a, b, preferred_element_type=F32)  21.1 us
    dot_general x7, matrix products, dot_t(): lax.dot_general(a, b, (((1,), (1,)), ((), ())), preferred_element_type=F32)  20.7 us
    psum x1, waiting for transfers between devices, body(): grad_normed = lax.psum(dot_t(grad_act, enc_in).astype(BF), 'mp').astype(F32)  17.9 us
    all_gather x1, waiting for transfers between devices, body(): lax.all_gather(lax.all_gather(grad_own, 'tile'), ('segment', 'mp'))  17.4 us
  transfers between devices with their start and end apart: 8, of which 7 were waited for; matrix products, arithmetic and copies ran while one was open for 6% of the time, Pallas kernels for 0%

profile of v1, /device:TPU:0, one launch (start us, length us, event | category | flops | bytes accessed | tf_op | source)
XLA Modules:
  0.0 331.8 jit_solution(18238731493559589069)
XLA Ops:
  7.2 1.4 convolution_convert_fusion.5
  8.6 0.2 reshape.254
  8.8 0.7 fusion.49
  9.4 0.1 all_gather_reshape.3
  9.6 15.0 %all_gather.25 = bf16[4,16,768]{2,1,0:T(8,128)(2,1)S(1)} all-gather(bf16[1,16,768]{2,1,0:T(8,128)(2,1)S(1)} %all_gather_reshape.3), channel_id=1, replica_groups=mesh['groups'=2,'tile'=4,'segment'=2,'mp'=2] {'tile'}, dimensions={0}, use_global_device_ids=true | all-gather | bytes 122880 | tf_op jit(solution)/shard_map/all_gather | solution.py:67
  24.7 0.1 multiply_reduce_fusion.2
  25.0 0.1 rsqrt.35
  25.2 2.2 fusion.50
  27.4 0.7 copy-done.3
  28.2 1.2 convolution_convert_fusion.4
  29.5 13.3 %all-gather.2 = bf16[4,4,2048]{2,1,0:T(4,128)(2,1)S(1)} all-gather(bf16[1,4,2048]{2,1,0:T(4,128)(2,1)S(1)} %bitcast.88), channel_id=1, replica_groups=mesh['groups'=2,'tile'=4,'segment'=2,'mp'=2] {'tile'}, dimensions={0}, use_global_device_ids=true | all-gather | bytes 81920 | tf_op jit(solution)/shard_map/all_gather | solution.py:69
  42.8 2.8 convolution_convert_fusion
  45.7 0.7 convert_element_type.165
  46.4 8.4 %all_gather.27 = bf16[512,672]{0,1:T(8,128)(2,1)S(1)} all-gather(bf16[512,336]{0,1:T(8,128)(2,1)} %param.19), channel_id=1, replica_groups=mesh['groups'=2,'tile'=4,'segment'=2,'mp'=2] {'mp'}, dimensions={1}, use_global_device_ids=true | all-gather | bytes 1032192 | tf_op jit(solution)/shard_map/all_gather | solution.py:70
  54.7 1.0 add_convert_fusion.2
  55.8 0.3 dot_general.61
  56.1 4.2 %multiply_reduce_fusion.1 = (f32[64,16]{1,0:T(8,128)S(1)}, bf16[64,16,2048]{2,1,0:T(8,128)(2,1)}) fusion(f32[16,2048]{1,0:T(8,128)} %convert_element_type.165, bf16[64,16,48]{2,1,0:T(8,128)(2,1)S(1)} %dot_general.61, bf16[48,2048]{1,0:T(8,128)(2,1)} %param.15), kind=kOutput, calls=%fused_computation.7 | convolution fusion | flops 211811328 | bytes 4624384 | tf_op jit(solution)/shard_map/dot_general | solution.py:33
  60.4 29.6 %all-reduce.8.cloned.1.call-done = bf16[64,2048]{1,0:T(8,128)(2,1)} async-done(((bf16[64,2048]{1,0:T(8,128)(2,1)}), bf16[64,2048]{1,0:T(8,128)(2,1)}) %all-reduce.8.cloned.1.call-update) | async-done | bytes 262160 | tf_op jit(solution)/shard_map/psum | solution.py:75
  90.0 0.8 slice_convert_fusion
  90.8 2.2 convolution_add_fusion
  93.0 5.3 %multiply_convert_fusion.1 = bf16[1024,2048]{1,0:T(8,128)(2,1)} fusion(f32[64,16,2048]{2,1,0:T(8,128)S(1)} %convolution_add_fusion, f32[1024]{0:T(1024)S(1)} %rsqrt.37), kind=kLoop, calls=%fused_computation.3 | loop fusion | flops 20971520 | bytes 12587008 | tf_op jit(solution)/shard_map/convert_element_type | solution.py:96
  98.3 7.2 %convolution_convert_fusion.1 = bf16[1024,672]{0,1:T(8,128)(2,1)} fusion(bf16[512,672]{0,1:T(8,128)(2,1)S(1)} %all_gather.27, bf16[1024,2048]{1,0:T(8,128)(2,1)} %multiply_convert_fusion.1, bf16[4096,512]{1,0:T(8,128)(2,1)} %param.18, s32[]{:T(128)S(6)} %select_n.37, bf16[1024,2048]{1,0:T(8,128)(2,1)} %bitcast.90, s32[]{:T(128)S(6)} %select_n.36, ...), kind=kOutput, calls=%fused_computation.22 | convolution fusion | flops 2854912000 | bytes 9404428 | tf_op jit(solution)/shard_map/dot_general | solution.py:33
  105.5 2.6 copy.40
  108.2 28.0 %reduce-scatter.3.cloned.1.call-done = bf16[1,4,64,672]{3,2,1,0:T(8,128)(2,1)} async-done(((bf16[4,4,64,672]{3,2,1,0:T(8,128)(2,1)}), bf16[1,4,64,672]{3,2,1,0:T(8,128)(2,1)}) %reduce-scatter.3.cloned.1.call-update) | async-done | bytes 344080 | tf_op jit(solution)/shard_map/reduce_scatter | solution.py:98
  136.6 0.1 lt.54
  136.7 0.2 copy.49
  136.9 1.8 copy.42
  138.7 1.9 reshape.268
  140.7 0.6 convert_reduce_fusion
  142.0 17.0 %reduce-scatter.5.cloned.1.call-done = bf16[1,64,672]{2,1,0:T(8,128)(2,1)} async-done(((bf16[4,64,672]{2,1,0:T(8,128)(2,1)}), bf16[1,64,672]{2,1,0:T(8,128)(2,1)}) %reduce-scatter.5.cloned.1.call-update) | async-done | bytes 86032 | tf_op jit(solution)/shard_map/reduce_scatter | solution.py:101
  159.0 1.0 multiply_convert_fusion.6
  160.0 15.8 %all_gather.28 = bf16[4,64,672]{2,1,0:T(8,128)(2,1)} all-gather(bf16[1,64,672]{2,1,0:T(8,128)(2,1)S(1)} %multiply_convert_fusion.6), channel_id=1, replica_groups=mesh['groups'=2,'tile'=4,'segment'=2,'mp'=2] {'tile'}, dimensions={0}, use_global_device_ids=true | all-gather | bytes 430080 | tf_op jit(solution)/shard_map/all_gather | solution.py:116
  175.8 0.2 all-reduce.10.cloned.1.call-start
  176.0 17.4 %all-gather.6.cloned.1.call-done = bf16[16,64,672]{2,1,0:T(8,128)(2,1)} async-done(((bf16[4,64,672]{2,1,0:T(8,128)(2,1)}), bf16[16,64,672]{2,1,0:T(8,128)(2,1)}) %all-gather.6.cloned.1.call-update) | async-done | bytes 1376272 | tf_op jit(solution)/shard_map/all_gather | solution.py:116
  193.4 2.7 convolution_convert_fusion.2
  196.1 0.2 copy-done.12
  196.3 9.2 %multiply_reduce_fusion = (f32[1024]{0:T(1024)S(1)}, bf16[1024,2048]{1,0:T(8,128)(2,1)S(1)}) fusion(f32[64,16,2048]{2,1,0:T(8,128)} %copy-done.1, f32[1024]{0:T(1024)S(1)} %rsqrt.37, bf16[1024,512]{1,0:T(8,128)(2,1)S(1)} %convolution_convert_fusion.2, bf16[4096,512]{1,0:T(8,128)(2,1)S(1)} %copy-done.12, s32[]{:T(128)S(6)} %select_n.37), kind=kOutput, calls=%fused_computation.1 | convolution fusion | flops 2191522816 | bytes 15736836 | tf_op jit(solution)/shard_map/dot_general | solution.py:37
  205.5 0.4 convolution_multiply_fusion.1
  206.0 1.5 fusion.20
  207.5 2.0 fusion.21
  209.5 1.1 copy.43
  210.6 0.9 convert_element_type.188
  211.6 0.2 multiply_reduce_fusion.3
  211.8 31.1 %all-reduce.10.cloned.1.call-done = bf16[64,768]{1,0:T(8,128)(2,1)} async-done(((bf16[64,768]{1,0:T(8,128)(2,1)}), bf16[64,768]{1,0:T(8,128)(2,1)}) %all-reduce.10.cloned.1.call-update) | async-done | bytes 98320 | tf_op jit(solution)/shard_map/psum | solution.py:126
  243.0 1.0 reshape.270
  244.1 35.4 %all-reduce.12.cloned.1.call-done = bf16[64,768]{1,0:T(8,128)(2,1)} async-done(((bf16[64,768]{1,0:T(8,128)(2,1)}), bf16[64,768]{1,0:T(8,128)(2,1)}) %all-reduce.12.cloned.1.call-update) | async-done | bytes 98320 | tf_op jit(solution)/shard_map/psum | solution.py:127
  279.5 1.7 fusion.4
  281.2 3.1 convolution_convert_fusion.3
  284.4 1.9 fusion.36
  286.3 0.9 reshape.261
  287.2 0.7 copy.45
  287.9 1.9 fusion.34
  289.8 0.9 reshape.260
  290.8 0.1 reshape.269
  290.9 17.9 %all-reduce.14.cloned.1.call-done = bf16[4,4,4,768]{3,2,0,1:T(4,128)(2,1)} async-done(((bf16[4,4,4,768]{3,2,0,1:T(4,128)(2,1)}), bf16[4,4,4,768]{3,2,0,1:T(4,128)(2,1)}) %all-reduce.14.cloned.1.call-update) | async-done | bytes 98320 | tf_op jit(solution)/shard_map/psum | solution.py:133
  308.8 0.9 multiply_reduce_fusion.4
  309.7 0.1 div.44
  309.8 0.7 dynamic-slice_convert_fusion.1
  310.5 0.1 reshape.263
  310.6 0.1 fusion.30
  310.8 0.1 reshape.264
  310.9 0.1 convolution_bitcast_fusion
  311.0 13.3 %all-gather.3 = f32[4,224,16]{1,2,0:T(8,128)S(1)} all-gather(f32[1,224,16]{1,2,0:T(8,128)S(1)} %convolution_bitcast_fusion), channel_id=3, replica_groups=mesh['groups'=2,'tile'=4,'segment'=2,'mp'=2] {'tile'}, dimensions={0}, use_global_device_ids=true | all-gather | bytes 71680 | tf_op jit(solution)/shard_map/all_gather | solution.py:141
  324.3 0.7 constant_dynamic-slice_fusion
  (65 shorter events, 1.4 us)
Async XLA Ops:
  7.2 21.0 %copy-start = (bf16[1536,768]{1,0:T(8,128)(2,1)S(1)}, bf16[1536,768]{1,0:T(8,128)(2,1)}, u32[]{:S(2)}) copy-start(bf16[1536,768]{1,0:T(8,128)(2,1)} %param.14) | copy-start | bytes 7077892
  7.2 22.3 %copy-start.10 = (bf16[4,2048]{1,0:T(4,128)(2,1)S(1)}, bf16[4,2048]{1,0:T(4,128)(2,1)}, u32[]{:S(2)}) copy-start(bf16[4,2048]{1,0:T(4,128)(2,1)} %param.16) | copy-start | bytes 49156
  7.2 47.6 %all-reduce.6.cloned.1.call-start = ((), (), s32[]{:S(2)}) async-start(), calls=%async_computation.2 | async-start | bytes 196608 | tf_op jit(solution)/shard_map/psum | solution.py:81
  7.2 35.6 %copy-start.8 = (bf16[48,2048]{1,0:T(8,128)(2,1)S(1)}, bf16[48,2048]{1,0:T(8,128)(2,1)}, u32[]{:S(2)}) copy-start(bf16[48,2048]{1,0:T(8,128)(2,1)} %param.15) | copy-start | bytes 589828
  25.2 4.3 %copy-start.7 = (bf16[64,768]{1,0:T(8,128)(2,1)}, bf16[64,768]{1,0:T(8,128)(2,1)S(1)}, u32[]{:S(2)}) copy-start(bf16[64,768]{1,0:T(8,128)(2,1)S(1)} %multiply_convert_fusion.7) | copy-start | bytes 294916
  27.4 0.8 copy-start.3
  29.4 60.6 %all-reduce.8.cloned.1.call-start = ((), (), s32[]{:S(2)}) async-start(), calls=%async_computation.3 | async-start | bytes 524288 | tf_op jit(solution)/shard_map/psum | solution.py:75
  45.6 90.6 %reduce-scatter.3.cloned.1.call-start = ((), (), s32[]{:S(2)}) async-start(), calls=%async_computation.4 | async-start | bytes 1966080 | tf_op jit(solution)/shard_map/reduce_scatter | solution.py:98
  54.7 43.5 %copy-start.6 = (bf16[512,672]{0,1:T(8,128)(2,1)}, bf16[512,672]{0,1:T(8,128)(2,1)S(1)}, u32[]{:S(2)}) copy-start(bf16[512,672]{0,1:T(8,128)(2,1)S(1)} %all_gather.27) | copy-start | bytes 2064388
  93.0 5.3 %copy-start.1 = (f32[64,16,2048]{2,1,0:T(8,128)}, f32[64,16,2048]{2,1,0:T(8,128)S(1)}, u32[]{:S(2)}) copy-start(f32[64,16,2048]{2,1,0:T(8,128)S(1)} %convolution_add_fusion) | copy-start | bytes 25165828
  105.5 30.8 %copy-start.11 = (s32[2,32]{1,0:T(2,128)S(1)}, s32[2,32]{1,0:T(2,128)}, u32[]{:S(2)}) copy-start(s32[2,32]{1,0:T(2,128)} %param.11) | copy-start | bytes 772
  105.5 31.2 %copy-start.2 = (bf16[2,8,48,224]{3,2,1,0:T(8,128)(2,1)S(1)}, bf16[2,8,48,224]{3,2,1,0:T(8,128)(2,1)}, u32[]{:S(2)}) copy-start(bf16[2,8,48,224]{3,2,1,0:T(8,128)(2,1)} %param.10) | copy-start | bytes 1032196
  108.1 50.8 %reduce-scatter.5.cloned.1.call-start = ((), (), s32[]{:S(2)}) async-start(), calls=%async_computation.5 | async-start | bytes 491520 | tf_op jit(solution)/shard_map/reduce_scatter | solution.py:101
  136.2 57.2 %all-gather.6.cloned.1.call-start = ((), (), s32[]{:S(2)}) async-start(), calls=%async_computation.9 | async-start | bytes 1966080 | tf_op jit(solution)/shard_map/all_gather | solution.py:116
  175.8 67.1 %all-reduce.10.cloned.1.call-start = ((), (), s32[]{:S(2)}) async-start(), calls=%async_computation.6 | async-start | bytes 196608 | tf_op jit(solution)/shard_map/psum | solution.py:126
  193.4 2.9 copy-start.12
  196.3 9.2 %copy-start.9 = (bf16[48,2048]{1,0:T(8,128)(2,1)S(1)}, bf16[48,2048]{1,0:T(8,128)(2,1)}, u32[]{:S(2)}) copy-start(bf16[48,2048]{1,0:T(8,128)(2,1)} %param.15) | copy-start | bytes 589828
  196.3 9.7 %copy-start.13 = (bf16[64,16,2048]{2,1,0:T(8,128)(2,1)S(1)}, bf16[64,16,2048]{2,1,0:T(8,128)(2,1)}, u32[]{:S(2)}) copy-start(bf16[64,16,2048]{2,1,0:T(8,128)(2,1)} %get-tuple-element.6) | copy-start | bytes 12582916
  206.0 1.5 copy-start.5
  207.5 72.1 %copy-start.4 = (f32[64,1536]{1,0:T(8,128)S(1)}, f32[64,1536]{1,0:T(8,128)}, u32[]{:S(2)}) copy-start(f32[64,1536]{1,0:T(8,128)} %copy-done.3) | copy-start | bytes 1179652
  211.5 68.0 %all-reduce.12.cloned.1.call-start = ((), (), s32[]{:S(2)}) async-start(), calls=%async_computation.7 | async-start | bytes 196608 | tf_op jit(solution)/shard_map/psum | solution.py:127
  242.9 65.8 %all-reduce.14.cloned.1.call-start = ((), (), s32[]{:S(2)}) async-start(), calls=%async_computation.8 | async-start | bytes 196608 | tf_op jit(solution)/shard_map/psum | solution.py:133
Sparse Core Ops, SparseCore 0:
  29.5 22.1 all-reduce.5
  54.6 35.3 all-reduce.7
  108.3 27.9 reduce-scatter.2
  138.3 20.5 reduce-scatter.4
  175.9 17.4 all-gather.5
  211.6 31.2 all-reduce.9
  245.2 34.2 all-reduce.11
  288.0 20.6 all-reduce.13
